TPU v7x, 32 devices: a whole 2x2x4 slice. The times are simulated.
32 devices in a mesh: span: 16 (over z, x, core), section: 2 (over y).
Axes of the slice: x: 2, y: 2, z: 4, core: 2. Of those that a mesh axis runs over, the one named last changes fastest.
Arguments:
- clip_tokens: bfloat16 [2176, 1120], P('span'), may hold values from -6 to 6
- frame_ids: int32 [2176], P('span'), may hold values from 0 to 63, never falling along the last dimension, each value on 1 to 68 neighbouring positions
- norm_gain: float32 [2, 1120], P('section'), may hold values from 0.25 to 1.75
- qkv_weight: bfloat16 [2, 3763200], P('section', 'span'), may hold values from -0.1875 to 0.1875
- head_gain: float32 [2, 1120], P('section'), may hold values from 0.25 to 1.75
- out_weight: bfloat16 [2, 1254400], P('section', 'span'), may hold values from -0.1875 to 0.1875
Outputs:
- section_outputs: bfloat16 [2, 2176, 1120], P('section', 'span')
Inputs may be any that keep to these rules, and one draw needn't show every extreme that they name: `frame_ids`: frame numbers never fall along the clip.
All inputs are finite; a program needn't handle non-finite values.
Results may differ from a plain program's by a relative error of at most 0.0064.
Values may be sent and summed in bfloat16 or wider, within the bound.
A program may use at most 64 MiB of HBM per device.

v0:
```python
import jax
import jax.numpy as jnp
from jax import lax
from jax.sharding import PartitionSpec as P

HEAD = 112


def shifted(block, axis, distance):
    devices = range(lax.axis_size(axis))
    route = [(i - distance, i) for i in devices if i - distance in devices]
    return lax.ppermute(block, axis, route)


def on_device(clip_tokens, frame_ids, norm_gain, qkv_weight, head_gain, out_weight):
    row_count = clip_tokens.shape[0]
    model_width = clip_tokens.shape[1]
    qkv_flat, out_flat = (
        lax.all_gather(qkv_weight, "span", axis=1, tiled=True),
        lax.all_gather(out_weight, "span", axis=1, tiled=True),
    )
    w_qkv = qkv_flat.reshape(model_width, -1)
    inner_width = w_qkv.shape[1] // 3
    w_out = out_flat.reshape(inner_width, model_width)
    head_count = inner_width // HEAD
    norm_scale = norm_gain[0]
    head_scale = head_gain[0].reshape(head_count, HEAD)
    allowed = frame_ids[None, :] <= frame_ids[:, None]
    section_count = lax.axis_size("section")
    span_count = lax.axis_size("span")
    my_section = lax.axis_index("section")

    def project(current):
        current_wide = current.astype(jnp.float32)
        normed = (
            current_wide
            * lax.rsqrt(jnp.mean(current_wide * current_wide, axis=1, keepdims=True) + 1e-06)
            * norm_scale
        ).astype(jnp.bfloat16)
        projected = jnp.dot(normed, w_qkv, preferred_element_type=jnp.float32)
        queries = (
            jnp.maximum(projected[:, :inner_width], 0.0)
            .astype(jnp.bfloat16)
            .reshape(row_count, head_count, HEAD)
        )
        key_feats = (
            jnp.maximum(projected[:, inner_width : 2 * inner_width], 0.0)
            .astype(jnp.bfloat16)
            .reshape(row_count, head_count, HEAD)
        )
        value_rows = (
            projected[:, 2 * inner_width :]
            .astype(jnp.bfloat16)
            .reshape(row_count, head_count, HEAD)
        )
        span_state = jnp.einsum(
            "jhd,jhe->hde", key_feats, value_rows, preferred_element_type=jnp.float32
        )
        return (queries, key_feats, value_rows, span_state)

    def local_term(queries, key_feats, value_rows):
        scores = jnp.einsum("ihd,jhd->hij", queries, key_feats, preferred_element_type=jnp.float32)
        weights = jnp.where(allowed[None, :, :], scores, 0.0).astype(jnp.bfloat16)
        return jnp.einsum("hij,jhd->ihd", weights, value_rows, preferred_element_type=jnp.float32)

    def finish(current, queries, local_part, carried):
        mixture = local_part + jnp.einsum(
            "ihd,hde->ihe", queries, carried, preferred_element_type=jnp.float32
        )
        attended = (
            mixture
            * lax.rsqrt(jnp.mean(mixture * mixture, axis=2, keepdims=True) + 1e-06)
            * head_scale
        ).astype(jnp.bfloat16)
        attended = attended.reshape(row_count, inner_width)
        return (
            current.astype(jnp.float32)
            + jnp.dot(attended, w_out, preferred_element_type=jnp.float32)
        ).astype(jnp.bfloat16)

    def prefix(span_state):
        sliced = span_state.reshape(span_count, -1)
        owned = lax.all_to_all(sliced, "span", split_axis=0, concat_axis=0, tiled=True)
        running = jnp.cumsum(owned, axis=0)
        earlier = (running - owned).astype(jnp.bfloat16)
        returned = lax.all_to_all(earlier, "span", split_axis=0, concat_axis=0, tiled=True)
        return returned.reshape(span_state.shape)

    empty_heads = jnp.zeros((row_count, head_count, HEAD), jnp.bfloat16)
    empty_state = jnp.zeros((head_count, HEAD, HEAD), jnp.float32)

    def step(step_index, loop_state):
        current, result = loop_state
        active = my_section == step_index

        def early_on(operand):
            return project(operand)

        def early_off(operand):
            return (empty_heads, empty_heads, empty_heads, empty_state)

        queries, key_feats, value_rows, span_state = lax.cond(active, early_on, early_off, current)
        carried = prefix(span_state)

        def late_on(operands):
            local_part = local_term(operands[1], operands[2], operands[3])
            return finish(operands[0], operands[1], local_part, operands[4])

        def late_off(operands):
            return jnp.zeros_like(operands[0])

        updated = lax.cond(
            active, late_on, late_off, (current, queries, key_feats, value_rows, carried)
        )
        result = jnp.where(active, updated, result)
        arrived = shifted(updated, "section", 1)
        return (arrived, result)

    initial = (clip_tokens, jnp.zeros_like(clip_tokens))
    final_state = lax.fori_loop(0, section_count, step, initial)
    return final_state[1][None, :, :]


def solution(mesh):
    return jax.shard_map(
        on_device,
        mesh=mesh,
        in_specs=(
            P("span", None),
            P("span"),
            P("section", None),
            P("section", "span"),
            P("section", None),
            P("section", "span"),
        ),
        out_specs=P("section", "span", None),
        check_vma=False,
    )
```

profile of v0, /device:TPU:5, one launch (start us, length us, event | category | flops | bytes accessed | tf_op | source)
XLA Modules:
  0.0 415.3 jit_solution(5132505690820584310)
XLA Ops:
  6.5 1.2 dynamic-slice
  9.1 8.9 %reduce.3 = bf16[235200]{0:T(1024)(128)(2,1)S(1)} reduce(bf16[1,235200]{1,0:T(2,128)(2,1)} %param.15, bf16[]{:T(256)} %constant.68), dimensions={0}, to_apply=%param.15.reduce_sub_computation | reduce | bytes 940802 | tf_op args[3]
  18.0 1.8 reduce.4
  19.8 3.4 broadcast.47
  23.2 8.2 %dynamic-update-slice = bf16[3763200]{0:T(1024)(128)(2,1)} dynamic-update-slice(bf16[3763200]{0:T(1024)(128)(2,1)} %broadcast.47, bf16[235200]{0:T(1024)(128)(2,1)S(1)} %reduce.3, u32[]{:T(128)} %bitcast.2) | dynamic-update-slice | bytes 940804
  31.5 1.5 dynamic-update-slice.1
  33.0 1.4 copy-done.1
  34.5 196.9 %all-reduce.5.cloned.1.call-done = (bf16[3763200]{0:T(1024)(128)(2,1)}, bf16[1254400]{0:T(1024)(128)(2,1)}) async-done(((bf16[3763200]{0:T(1024)(128)(2,1)}, bf16[1254400]{0:T(1024)(128)(2,1)}), (bf16[3763200]{0:T(1024)(128)(2,1)}, bf16[1254400]{0:T(1024)(128)(2,1)})) %all-reduce.5.cloned.1.call-update) | async-done | bytes 10035216
  231.4 15.5 %reshape.60 = bf16[1120,3360]{1,0:T(8,128)(2,1)} reshape(bf16[3763200]{0:T(1024)(128)(2,1)} %get-tuple-element.280) | data formatting | bytes 15052800 | tf_op jit(solution)/shard_map/reshape | solution.py:22
  246.9 5.1 %reshape.61 = bf16[1120,1120]{1,0:T(8,128)(2,1)S(1)} reshape(bf16[1254400]{0:T(1024)(128)(2,1)} %get-tuple-element.281) | data formatting | bytes 5017600 | tf_op jit(solution)/shard_map/reshape | solution.py:24
  252.0 156.5 %while.16 = (s32[]{:T(128)}, bf16[136,1120]{1,0:T(8,128)(2,1)S(1)}, bf16[136,1120]{1,0:T(8,128)(2,1)}, s32[]{:T(128)}, f32[1,1120]{1,0:T(1,128)S(1)}, /*index=5*...) while((s32[]{:T(128)}, bf16[136,1120]{1,0:T(8,128)(2,1)S(1)}, ...), condition=%wide.region_8.9_spmd.clone, body=%wide.region_0.8_spmd.clone.sunk | while | flops 1522066688 | bytes 30926768 | solution.py:120
  252.2 2.8 conditional.6
  252.3 0.9 broadcast_in_dim.12
  253.2 0.9 broadcast_in_dim.12.clone
  255.0 1.7 all_to_all.24
  256.7 18.6 %all_to_all.29 = f32[16,1,7840]{2,1,0:T(1,128)S(1)} all-to-all(f32[16,1,7840]{2,1,0:T(1,128)} %all_to_all.24), channel_id=1, replica_groups=mesh['span'=16,'section'=2] {'span'}, dimensions={0} | all-to-all | bytes 1003520 | tf_op jit(solution)/shard_map/while/body/eval_jaxpr/all_to_all | solution.py:83
  276.3 3.0 reduce.7
  279.3 1.9 reshape.84
  281.2 4.5 %all-to-all-start.1 = ((bf16[16,2,3920]{2,1,0:T(2,128)(2,1)}), bf16[16,2,3920]{2,1,0:T(2,128)(2,1)}, u32[]{:S(2)}, u32[]{:S(2)}) async-start(bf16[16,2,3920]{2,1,0:T(2,128)(2,1)} %reshape.84), calls=%async_computation.1 | async-start | bytes 507904 | tf_op jit(solution)/shard_map/while/body/eval_jaxpr/all_to_all | solution.py:86
  285.6 9.5 %all-to-all-done.1 = bf16[16,2,3920]{2,1,0:T(2,128)(2,1)} async-done(((bf16[16,2,3920]{2,1,0:T(2,128)(2,1)}), bf16[16,2,3920]{2,1,0:T(2,128)(2,1)}, u32[]{:S(2)}, u32[]{:S(2)}) %all-to-all-start.1) | async-done | bytes 250912 | tf_op jit(solution)/shard_map/while/body/eval_jaxpr/all_to_all | solution.py:86
  295.1 1.3 reshape.85
  297.2 1.3 collective-permute-start
  299.2 30.6 %collective-permute-done = bf16[136,1120]{1,0:T(8,128)(2,1)S(1)} collective-permute-done((bf16[136,1120]{1,0:T(8,128)(2,1)}, bf16[136,1120]{1,0:T(8,128)(2,1)S(1)}, u32[]{:S(2)}, u32[]{:S(2)}) %collective-permute-start) | collective-permute-done | bytes 304672 | tf_op jit(solution)/shard_map/while/body/eval_jaxpr/ppermute | solution.py:12
  329.8 13.0 %conditional.6 = (bf16[136,10,112]{2,1,0:T(8,128)(2,1)}, bf16[136,10,112]{2,1,0:T(8,128)(2,1)}, bf16[136,10,112]{2,1,0:T(8,128)(2,1)}, f32[10,112,112]{2,1,0:T(8,128)S(1)}) conditional(s32[]{:T(128)} %convert_element_type.68, () %tuple.60, (bf16[136,1120]{1,0:T(8,128)(2,1)S(1)}, f32[1,1120]{1,0:T(1,128)S(1)}, bf16[1120,3360]{1,0:T(8,128)(2,1)}) %tuple.61), branch_computations={%region_1.0_spmd, %region_2.0_spmd} | conditional | flops 1059690368 | bytes 13831972 | solution.py:102
  330.0 4.7 %fusion.10 = bf16[136,3360]{1,0:T(8,128)(2,1)S(1)} fusion(bf16[1120,3360]{1,0:T(8,128)(2,1)} %get-tuple-element.180, bf16[136,1120]{1,0:T(8,128)(2,1)S(1)} %get-tuple-element.178, f32[1120]{0:T(1024)S(1)} %reduce, f32[136]{0:T(256)S(1)} %add_rsqrt_fusion), kind=kOutput, calls=%fused_computation.14 | convolution fusion | flops 1024199680 | bytes 8749984 | tf_op jit(solution)/shard_map/while/body/eval_jaxpr/cond/branch_1_fun/dot_general | solution.py:40
  334.7 1.0 fusion.27
  335.7 1.5 reshape.54
  337.2 1.5 reshape.55
  338.7 1.6 fusion.7
  340.3 2.5 reshape.53
  342.8 1.7 all_to_all.24
  344.5 18.4 %all_to_all.29 = f32[16,1,7840]{2,1,0:T(1,128)S(1)} all-to-all(f32[16,1,7840]{2,1,0:T(1,128)} %all_to_all.24), channel_id=1, replica_groups=mesh['span'=16,'section'=2] {'span'}, dimensions={0} | all-to-all | bytes 1003520 | tf_op jit(solution)/shard_map/while/body/eval_jaxpr/all_to_all | solution.py:83
  363.9 3.0 reduce.7
  366.9 1.9 reshape.84
  368.7 4.4 %all-to-all-start.1 = ((bf16[16,2,3920]{2,1,0:T(2,128)(2,1)}), bf16[16,2,3920]{2,1,0:T(2,128)(2,1)}, u32[]{:S(2)}, u32[]{:S(2)}) async-start(bf16[16,2,3920]{2,1,0:T(2,128)(2,1)} %reshape.84), calls=%async_computation.1 | async-start | bytes 507904 | tf_op jit(solution)/shard_map/while/body/eval_jaxpr/all_to_all | solution.py:86
  373.1 9.5 %all-to-all-done.1 = bf16[16,2,3920]{2,1,0:T(2,128)(2,1)} async-done(((bf16[16,2,3920]{2,1,0:T(2,128)(2,1)}), bf16[16,2,3920]{2,1,0:T(2,128)(2,1)}, u32[]{:S(2)}, u32[]{:S(2)}) %all-to-all-start.1) | async-done | bytes 250912 | tf_op jit(solution)/shard_map/while/body/eval_jaxpr/all_to_all | solution.py:86
  382.6 1.3 reshape.85
  383.8 14.3 %conditional.7 = (bf16[136,1120]{1,0:T(8,128)(2,1)}) conditional(s32[]{:T(128)} %convert_element_type.68, () %tuple.59, (bf16[136,1120]{1,0:T(8,128)(2,1)S(1)}, s32[136]{0:T(256)S(1)}, bf16[136,10,112]{2,1,0:T(8,128)(2,1)}, bf16[136,10,112]{2,1,0:T(8,128)(2,1)}, bf16[136,10,112]{2,1,0:T(8,128)(2,1)}, /*index=5*/bf16[16,1,7840]{2,1,0:T(2,128)(2,1)S(1)}, ...), branch_computations={%region_5.5_spmd, %region_6.7_spmd} | conditional | flops 459939200 | bytes 9938254 | solution.py:112
  383.9 2.3 reduce.1
  386.2 1.5 reshape.56
  387.6 2.3 convolution_bitcast_fusion.1
  390.0 3.1 multiply_reduce_fusion
  393.2 1.4 multiply_convert_fusion
  394.6 1.1 reshape.57
  395.8 2.3 fusion.14
  398.1 1.3 collective-permute-start
  399.4 1.8 select_select_fusion.2
  401.3 7.2 %collective-permute-done = bf16[136,1120]{1,0:T(8,128)(2,1)S(1)} collective-permute-done((bf16[136,1120]{1,0:T(8,128)(2,1)}, bf16[136,1120]{1,0:T(8,128)(2,1)S(1)}, u32[]{:S(2)}, u32[]{:S(2)}) %collective-permute-start) | collective-permute-done | bytes 304672 | tf_op jit(solution)/shard_map/while/body/eval_jaxpr/ppermute | solution.py:12
  (30 shorter events, 6.0 us)
Async XLA Ops:
  6.5 224.9 %all-reduce.5.cloned.1.call-start = ((), (), s32[]{:S(2)}) async-start(), calls=%async_computation.2 | async-start | bytes 20070400
  33.0 1.4 copy-start.1
  246.9 5.1 %copy-start = (bf16[136,1120]{1,0:T(8,128)(2,1)S(1)}, bf16[136,1120]{1,0:T(8,128)(2,1)}, u32[]{:S(2)}) copy-start(bf16[136,1120]{1,0:T(8,128)(2,1)} %param.12) | copy-start | bytes 913924
  246.9 5.1 %copy-start.2 = (f32[1,1120]{1,0:T(1,128)S(1)}, f32[1,1120]{1,0:T(1,128)}, u32[]{:S(2)}) copy-start(f32[1,1120]{1,0:T(1,128)} %param.14) | copy-start | bytes 13444
  246.9 5.1 %copy-start.3 = (f32[1,1120]{1,0:T(1,128)S(1)}, f32[1,1120]{1,0:T(1,128)}, u32[]{:S(2)}) copy-start(f32[1,1120]{1,0:T(1,128)} %param.16) | copy-start | bytes 13444
  246.9 5.1 %copy-start.4 = (s32[136]{0:T(256)S(1)}, s32[136]{0:T(256)}, u32[]{:S(2)}) copy-start(s32[136]{0:T(256)} %param.13) | copy-start | bytes 1636
  281.2 13.9 %all-to-all-start.1 = ((bf16[16,2,3920]{2,1,0:T(2,128)(2,1)}), bf16[16,2,3920]{2,1,0:T(2,128)(2,1)}, u32[]{:S(2)}, u32[]{:S(2)}) async-start(bf16[16,2,3920]{2,1,0:T(2,128)(2,1)} %reshape.84), calls=%async_computation.1 | async-start | bytes 507904 | tf_op jit(solution)/shard_map/while/body/eval_jaxpr/all_to_all | solution.py:86
  297.2 32.6 %collective-permute-start = (bf16[136,1120]{1,0:T(8,128)(2,1)}, bf16[136,1120]{1,0:T(8,128)(2,1)S(1)}, u32[]{:S(2)}, u32[]{:S(2)}) collective-permute-start(bf16[136,1120]{1,0:T(8,128)(2,1)} %get-tuple-element.396), channel_id=1, source_target_pairs={{0,1},{2,3},{4,5},{6,7},{8,9},{10,11},{12,13},{14,15},{16,17},{18,... | collective-permute-start | bytes 913928 | tf_op jit(solution)/shard_map/while/body/eval_jaxpr/ppermute | solution.py:12
  368.7 13.8 %all-to-all-start.1 = ((bf16[16,2,3920]{2,1,0:T(2,128)(2,1)}), bf16[16,2,3920]{2,1,0:T(2,128)(2,1)}, u32[]{:S(2)}, u32[]{:S(2)}) async-start(bf16[16,2,3920]{2,1,0:T(2,128)(2,1)} %reshape.84), calls=%async_computation.1 | async-start | bytes 507904 | tf_op jit(solution)/shard_map/while/body/eval_jaxpr/all_to_all | solution.py:86
  398.1 10.4 %collective-permute-start = (bf16[136,1120]{1,0:T(8,128)(2,1)}, bf16[136,1120]{1,0:T(8,128)(2,1)S(1)}, u32[]{:S(2)}, u32[]{:S(2)}) collective-permute-start(bf16[136,1120]{1,0:T(8,128)(2,1)} %get-tuple-element.396), channel_id=1, source_target_pairs={{0,1},{2,3},{4,5},{6,7},{8,9},{10,11},{12,13},{14,15},{16,17},{18,... | collective-permute-start | bytes 913928 | tf_op jit(solution)/shard_map/while/body/eval_jaxpr/ppermute | solution.py:12
Sparse Core Ops, SparseCore 0:
  34.6 196.7 all-reduce.4
where the time goes:
time: 419 us; the launch traced here: 415 us
  waiting for transfers between devices  254 us (61%)
  local copies, waits for them, and re-layouts  59.1 us (14%)
  blocking collectives  37 us (9%)
  other arithmetic  25.1 us (6%)
  between operations  14.8 us (4%)
  matrix products  14 us (3%)
  starting transfers between devices  11.4 us (3%)
    unnamed x2, waiting for transfers between devices  197 us
    ppermute x2, waiting for transfers between devices, shifted(): return lax.ppermute(block, axis, route)  37.8 us
    all_to_all x2, blocking collectives, prefix(): lax.all_to_all(sliced, 'span', split_axis=0, concat_axis=0, tiled=True)  37 us
    all_to_all x2, waiting for transfers between devices, prefix(): lax.all_to_all(earlier, 'span', split_axis=0, concat_axis=0, tiled=True)  18.9 us
    unnamed x15, local copies, waits for them, and re-layouts  15.9 us
    reshape x1, local copies, waits for them, and re-layouts, on_device(): w_qkv = qkv_flat.reshape(model_width, -1)  15.5 us
    unnamed x3, other arithmetic  10.7 us
    all_to_all x2, starting transfers between devices, prefix(): lax.all_to_all(earlier, 'span', split_axis=0, concat_axis=0, tiled=True)  8.86 us
  transfers between devices with their start and end apart: 5, of which 5 were waited for; matrix products, arithmetic and copies ran while one was open for 1% of the time, Pallas kernels for 0%

commit v1 on v0

--- a/solution.py
+++ b/solution.py
@@ -1,9 +1,13 @@
 import jax
 import jax.numpy as jnp
 from jax import lax
+from jax.experimental import pallas as pl
+from jax.experimental.pallas import tpu as pltpu
 from jax.sharding import PartitionSpec as P
 
 HEAD = 112
+LANES = 128
+EPS = 1e-06
 
 
 def shifted(block, axis, distance):
@@ -121,9 +125,419 @@
     return final_state[1][None, :, :]
 
 
+def whole_tiles(count, tile):
+    return -(-count // tile) * tile
+
+
+def remote(src, dst, send, recv, span, section):
+    return pltpu.make_async_remote_copy(
+        src_ref=src,
+        dst_ref=dst,
+        send_sem=send,
+        recv_sem=recv,
+        device_id={"span": span, "section": section},
+        device_id_type=pl.DeviceIdType.MESH,
+    )
+
+
+def spread(size_in, size_out, group_in, kept_in, group_out, kept_out):
+    row = lax.broadcasted_iota(jnp.int32, (size_in, size_out), 0)
+    col = lax.broadcasted_iota(jnp.int32, (size_in, size_out), 1)
+    row_in, col_in = row % group_in, col % group_out
+    row_feature = row // group_in * kept_in + row_in
+    col_feature = col // group_out * kept_out + col_in
+    same = (row_feature == col_feature) & (row_in < kept_in) & (col_in < kept_out)
+    return jnp.where(same, 1.0, 0.0).astype(jnp.bfloat16)
+
+
+def layers_kernel(
+    x_ref, frame_ref, norm_ref, qkv_ref, head_ref, out_w_ref, y_ref,
+    held, packed, stream, normed, queries, keys, values, mixed, attended, fresh,
+    state, sent_state, got_state, sent_sum, got_sum,
+    frames, masks, norm_scale, head_scale, to_shards, from_heads,
+    gather_send, gather_recv, pair_send, pair_recv, state_send, state_recv,
+    sum_send, sum_recv, y_send, y_recv, local_sem,
+):
+    f32, bf16 = jnp.float32, jnp.bfloat16
+    span = lax.axis_index("span")
+    section = lax.axis_index("section")
+    core = span % 2
+    chip = span // 2
+    x_at = chip % 2
+    z_at = chip // 2
+    pair = span + 1 - 2 * core
+    x_near = span + 2 - 4 * x_at
+    chips = got_state.shape[0]
+    z_count = chips // 2
+    shards, shard_rows = held.shape[0], held.shape[1]
+    rows = x_ref.shape[0]
+    padded = stream.shape[1] // 2
+    half_width = x_ref.shape[1] // 2
+    half_lanes = stream.shape[2]
+    heads = half_width // HEAD
+    kept = qkv_ref.shape[0]
+    width = 2 * half_width
+
+    frames[...] = jnp.zeros_like(frames)
+    frames[pl.ds(core, 1), 0:1, 0:rows] = frame_ref[...].astype(f32)[None]
+
+    barrier = pltpu.get_barrier_semaphore()
+    for step in range(1, chips):
+        other = (chip + step) % chips * 2 + core
+        pl.semaphore_signal(
+            barrier, inc=1, device_id={"span": other, "section": section},
+            device_id_type=pl.DeviceIdType.MESH,
+        )
+    pl.semaphore_signal(
+        barrier, inc=1, device_id={"span": pair, "section": section},
+        device_id_type=pl.DeviceIdType.MESH,
+    )
+    pl.semaphore_signal(
+        barrier, inc=1, device_id={"span": span, "section": 1 - section},
+        device_id_type=pl.DeviceIdType.MESH,
+    )
+
+    packed[...] = jnp.zeros_like(packed)
+    for part in range(2):
+        for third in range(3):
+            for head in range(heads):
+                at = third * width + part * half_width + head * HEAD
+                to = (third * heads + head) * LANES
+                packed[part, 0:kept, to : to + HEAD] = qkv_ref[:, at : at + HEAD]
+        to = 3 * heads * LANES
+        packed[part, 0:kept, to : to + half_width] = out_w_ref[
+            :, part * half_width : (part + 1) * half_width
+        ]
+
+    pl.semaphore_wait(barrier, chips + 1)
+
+    own = pltpu.make_async_copy(packed.at[core], held.at[span], local_sem)
+    own.start()
+    give = remote(packed.at[1 - core], held.at[span], pair_send.at[0], gather_recv.at[span], pair, section)
+    give.start()
+    give_frames = remote(frames.at[core], frames.at[core], pair_send.at[1], pair_recv.at[1], pair, section)
+    give_frames.start()
+    own.wait()
+
+    def forward(lane, shard, target):
+        return remote(
+            held.at[shard], held.at[shard], gather_send.at[lane, shard], gather_recv.at[shard],
+            target, section,
+        )
+
+    def arrival(shard):
+        return remote(
+            held.at[shard], held.at[shard], gather_send.at[0, shard], gather_recv.at[shard],
+            pair, section,
+        )
+
+    def pass_on(step, from_core, first):
+        if step == 0:
+            shard = z_at * 4 + x_at * 2 + from_core
+            if not first:
+                arrival(shard).wait_recv()
+
+            @pl.when(z_at < z_count - 1)
+            def _():
+                forward(0, shard, span + 4).start()
+
+            @pl.when(z_at > 0)
+            def _():
+                forward(1, shard, span - 4).start()
+
+            forward(2, shard, x_near).start()
+        else:
+            below = (z_at - step) * 4 + x_at * 2 + from_core
+            above = (z_at + step) * 4 + x_at * 2 + from_core
+
+            @pl.when(z_at >= step)
+            def _():
+                arrival(below).wait_recv()
+
+                @pl.when(z_at < z_count - 1)
+                def _():
+                    forward(0, below, span + 4).start()
+
+                forward(2, below, x_near).start()
+
+            @pl.when(z_at + step < z_count)
+            def _():
+                arrival(above).wait_recv()
+
+                @pl.when(z_at > 0)
+                def _():
+                    forward(1, above, span - 4).start()
+
+                forward(2, above, x_near).start()
+
+    pass_on(0, core, True)
+    pass_on(0, 1 - core, False)
+
+    to_shards[...] = spread(half_lanes, half_lanes, half_lanes, half_width, shard_rows, kept)
+    from_heads[...] = spread(half_lanes, half_lanes, LANES, HEAD, shard_rows, kept)
+    norm_scale[...] = jnp.zeros_like(norm_scale)
+    for part in range(2):
+        norm_scale[part : part + 1, 0:half_width] = norm_ref[
+            :, part * half_width : (part + 1) * half_width
+        ]
+    head_scale[...] = jnp.zeros_like(head_scale)
+    for head in range(2 * heads):
+        head_scale[head : head + 1, 0:HEAD] = head_ref[:, head * HEAD : (head + 1) * HEAD]
+    give_frames.wait()
+    eye = lax.broadcasted_iota(jnp.int32, (padded, padded), 0) == lax.broadcasted_iota(
+        jnp.int32, (padded, padded), 1
+    )
+    for which in range(2):
+        along = jnp.broadcast_to(frames[which, 0:1, 0:padded], (padded, padded))
+        down = jnp.sum(jnp.where(eye, along, 0.0), axis=1, keepdims=True)
+        masks[which] = jnp.where(along <= down, 1.0, 0.0)
+
+    mine = pl.ds(pl.multiple_of(core * padded, 16), padded)
+    theirs = pl.ds(pl.multiple_of((1 - core) * padded, 16), padded)
+
+    @pl.when(section == 0)
+    def _():
+        fresh[...] = jnp.zeros_like(fresh)
+        for part in range(2):
+            fresh[part, 0:rows, 0:half_width] = x_ref[
+                :, part * half_width : (part + 1) * half_width
+            ]
+        put = pltpu.make_async_copy(fresh, stream.at[:, mine, :], local_sem)
+        put.start()
+        share = remote(fresh, stream.at[:, mine, :], pair_send.at[2], pair_recv.at[2], pair, section)
+        share.start()
+        put.wait()
+        share.wait()
+
+    for step in range(1, z_count):
+        pass_on(step, core, False)
+        pass_on(step, 1 - core, False)
+
+    for z_from in range(z_count):
+        for from_core in range(2):
+            arrival(z_from * 4 + (1 - x_at) * 2 + from_core).wait_recv()
+
+    @pl.when(section == 1)
+    def _():
+        arrive = remote(
+            stream.at[core], stream.at[core], y_send, y_recv, span, 1 - section
+        )
+        arrive.wait_recv()
+        share = remote(
+            stream.at[core], stream.at[core], pair_send.at[2], pair_recv.at[2], pair, section
+        )
+        share.start()
+        share.wait()
+
+    wide = [stream[part].astype(f32) for part in range(2)]
+    square = sum(jnp.sum(value * value, axis=1, keepdims=True) for value in wide)
+    inverse = lax.rsqrt(square / width + EPS)
+    for part in range(2):
+        scaled = (wide[part] * inverse * norm_scale[part : part + 1, :]).astype(bf16)
+        normed[:, part * half_lanes : (part + 1) * half_lanes] = jnp.dot(
+            scaled, to_shards[...], preferred_element_type=f32
+        ).astype(bf16)
+    lanes = heads * LANES
+    depth = shards * shard_rows
+    for third, into in ((1, keys), (2, values), (0, queries)):
+        weight = held[:, :, third * lanes : (third + 1) * lanes].reshape(depth, lanes)
+        result = jnp.dot(normed[...], weight, preferred_element_type=f32)
+        into[...] = (result if third == 2 else jnp.maximum(result, 0.0)).astype(bf16)
+
+    contract_rows = (((0,), (0,)), ((), ()))
+    for which in range(2):
+        at = slice(which * padded, (which + 1) * padded)
+        for head in range(heads):
+            cols = slice(head * LANES, (head + 1) * LANES)
+            state[which, cols, :] = lax.dot_general(
+                keys[at, cols], values[at, cols], contract_rows, preferred_element_type=f32
+            )
+    piece = sent_state.shape[1]
+    sent_state[...] = (state[0] + state[1]).astype(bf16).reshape(chips, piece, LANES)
+
+    def exchange(source, target, sends, recvs, step):
+        other = (chip + step) % chips
+        return remote(
+            source.at[other], target.at[chip], sends.at[other], recvs.at[chip],
+            other * 2 + core, section,
+        )
+
+    def landed(target, sends, recvs, step):
+        other = (chip + step) % chips
+        return remote(
+            target.at[other], target.at[other], sends.at[other], recvs.at[other],
+            other * 2 + core, section,
+        )
+
+    for step in range(1, chips):
+        exchange(sent_state, got_state, state_send, state_recv, step).start()
+    got_state[pl.ds(chip, 1)] = sent_state[pl.ds(chip, 1)]
+
+    contract_lanes = (((1,), (1,)), ((), ()))
+
+    def local_part(which):
+        at = slice(which * padded, (which + 1) * padded)
+        for head in range(heads):
+            cols = slice(head * LANES, (head + 1) * LANES)
+            scores = lax.dot_general(
+                queries[at, cols], keys[at, cols], contract_lanes, preferred_element_type=f32
+            )
+            scores = jnp.where(masks[which] > 0.5, scores, 0.0).astype(bf16)
+            mixed[at, cols] = jnp.dot(scores, values[at, cols], preferred_element_type=f32)
+
+    local_part(0)
+    for step in range(1, chips):
+        landed(got_state, state_send, state_recv, step).wait_recv()
+    running = jnp.zeros((piece, LANES), f32)
+    for index in range(chips):
+        sent_sum[index] = running.astype(bf16)
+        running = running + got_state[index].astype(f32)
+    for step in range(1, chips):
+        exchange(sent_sum, got_sum, sum_send, sum_recv, step).start()
+    got_sum[pl.ds(chip, 1)] = sent_sum[pl.ds(chip, 1)]
+    local_part(1)
+    for step in range(1, chips):
+        landed(got_sum, sum_send, sum_recv, step).wait_recv()
+
+    carried = got_sum[...].reshape(lanes, LANES)
+    for which in range(2):
+        at = slice(which * padded, (which + 1) * padded)
+        for head in range(heads):
+            cols = slice(head * LANES, (head + 1) * LANES)
+            earlier = carried[cols, :]
+            if which == 1:
+                earlier = (earlier.astype(f32) + state[0, cols, :]).astype(bf16)
+            mixture = mixed[at, cols] + jnp.dot(
+                queries[at, cols], earlier, preferred_element_type=f32
+            )
+            size = jnp.sum(mixture * mixture, axis=1, keepdims=True) / HEAD
+            queries[at, cols] = (
+                mixture * lax.rsqrt(size + EPS) * head_scale[pl.ds(core * heads + head, 1), :]
+            ).astype(bf16)
+    fresh_heads = jnp.dot(queries[...], from_heads[...], preferred_element_type=f32)
+    attended[pl.ds(core, 1)] = fresh_heads.astype(bf16)[None]
+    swap = remote(attended.at[core], attended.at[core], pair_send.at[3], pair_recv.at[3], pair, section)
+    swap.start()
+    swap.wait()
+
+    half_depth = depth // 2
+    total = stream[pl.ds(core, 1)].astype(f32)[0]
+    for part in range(2):
+        weight = held[
+            part * (shards // 2) : (part + 1) * (shards // 2), :, 3 * lanes : 3 * lanes + half_lanes
+        ].reshape(half_depth, half_lanes)
+        total = total + jnp.dot(attended[part], weight, preferred_element_type=f32)
+    mixed_out = total.astype(bf16)
+    keys[...] = mixed_out
+
+    @pl.when(section == 0)
+    def _():
+        remote(keys, stream.at[core], y_send, y_recv, span, 1 - section).start()
+
+    back = remote(keys.at[theirs, :], y_ref.at[core], pair_send.at[4], pair_recv.at[4], pair, section)
+    back.start()
+    keep = pltpu.make_async_copy(keys.at[mine, :], y_ref.at[core], local_sem)
+    keep.start()
+    keep.wait()
+    back.wait()
+
+    @pl.when(section == 0)
+    def _():
+        remote(keys, stream.at[core], y_send, y_recv, span, 1 - section).wait_send()
+
+    give.wait_send()
+    for step in range(1, chips):
+        exchange(sent_state, got_state, state_send, state_recv, step).wait_send()
+        exchange(sent_sum, got_sum, sum_send, sum_recv, step).wait_send()
+    for z_from in range(z_count):
+        for from_core in range(2):
+            shard = z_from * 4 + x_at * 2 + from_core
+            forward(2, shard, x_near).wait_send()
+
+            @pl.when((z_from <= z_at) & (z_at < z_count - 1))
+            def _():
+                forward(0, shard, span + 4).wait_send()
+
+            @pl.when((z_from >= z_at) & (z_at > 0))
+            def _():
+                forward(1, shard, span - 4).wait_send()
+
+
+def fused(clip_tokens, frame_ids, norm_gain, qkv_weight, head_gain, out_weight):
+    shards = lax.axis_size("span")
+    rows, width = clip_tokens.shape
+    half_width = width // 2
+    kept = width // shards
+    heads = half_width // HEAD
+    shard_rows = whole_tiles(kept, 16)
+    padded = whole_tiles(rows, 16)
+    half_lanes = whole_tiles(half_width, LANES)
+    lanes = heads * LANES
+    chips = shards // 2
+    bf16, f32 = jnp.bfloat16, jnp.float32
+    dma = pltpu.SemaphoreType.DMA
+    vmem = pl.BlockSpec(memory_space=pltpu.VMEM)
+    y = pl.pallas_call(
+        layers_kernel,
+        out_shape=jax.ShapeDtypeStruct((2, padded, half_lanes), bf16),
+        in_specs=[vmem] * 6,
+        out_specs=vmem,
+        scratch_shapes=[
+            pltpu.VMEM((shards, shard_rows, 3 * lanes + half_lanes), bf16),
+            pltpu.VMEM((2, shard_rows, 3 * lanes + half_lanes), bf16),
+            pltpu.VMEM((2, 2 * padded, half_lanes), bf16),
+            pltpu.VMEM((2 * padded, shards * shard_rows), bf16),
+            pltpu.VMEM((2 * padded, lanes), bf16),
+            pltpu.VMEM((2 * padded, lanes), bf16),
+            pltpu.VMEM((2 * padded, lanes), bf16),
+            pltpu.VMEM((2 * padded, lanes), f32),
+            pltpu.VMEM((2, 2 * padded, half_lanes), bf16),
+            pltpu.VMEM((2, padded, half_lanes), bf16),
+            pltpu.VMEM((2, lanes, LANES), f32),
+            pltpu.VMEM((chips, lanes // chips, LANES), bf16),
+            pltpu.VMEM((chips, lanes // chips, LANES), bf16),
+            pltpu.VMEM((chips, lanes // chips, LANES), bf16),
+            pltpu.VMEM((chips, lanes // chips, LANES), bf16),
+            pltpu.VMEM((2, 8, whole_tiles(padded, LANES)), f32),
+            pltpu.VMEM((2, padded, padded), f32),
+            pltpu.VMEM((8, half_lanes), f32),
+            pltpu.VMEM((whole_tiles(2 * heads, 8), LANES), f32),
+            pltpu.VMEM((half_lanes, half_lanes), bf16),
+            pltpu.VMEM((lanes, half_lanes), bf16),
+            dma((3, shards)),
+            dma((shards,)),
+            dma((5,)),
+            dma((5,)),
+            dma((chips,)),
+            dma((chips,)),
+            dma((chips,)),
+            dma((chips,)),
+            dma,
+            dma,
+            dma,
+        ],
+        compiler_params=pltpu.CompilerParams(
+            collective_id=0, has_side_effects=True, vmem_limit_bytes=48 * 1024 * 1024
+        ),
+    )(
+        clip_tokens,
+        frame_ids.reshape(1, rows),
+        norm_gain,
+        qkv_weight.reshape(kept, -1),
+        head_gain,
+        out_weight.reshape(kept, width),
+    )
+    halves = y[:, :rows, :half_width]
+    return jnp.concatenate([halves[0], halves[1]], axis=1)[None]
+
+
+def grid_fits(mesh):
+    return mesh.shape["span"] == 16 and mesh.shape["section"] == 2
+
+
 def solution(mesh):
     return jax.shard_map(
-        on_device,
+        fused if grid_fits(mesh) else on_device,
         mesh=mesh,
         in_specs=(
             P("span", None),

time: 419 us -> 135 us (0.32)
  waiting for transfers between devices: 254 us -> 0 us
  Pallas kernels: 0 us -> 122 us
  local copies, waits for them, and re-layouts: 59.1 us -> 1.91 us
  blocking collectives: 37 us -> 0 us
  between operations: 14.8 us -> 0.08 us
  other arithmetic: 25.1 us -> 10.7 us
  matrix products: 14 us -> 0 us
  starting transfers between devices: 11.4 us -> 0 us
    unnamed x2 -> x0, waiting for transfers between devices: 197 us -> none
    pallas_call x0 -> x1, Pallas kernels: none -> 122 us  [fused(): pl.pallas_call(layers_kernel, out_shape=jax.ShapeDtypeStruct((2, padded,...]
    ppermute x2 -> x0, waiting for transfers between devices: 37.8 us -> none  [shifted(): return lax.ppermute(block, axis, route)]
    all_to_all x2 -> x0, blocking collectives: 37 us -> none  [prefix(): lax.all_to_all(sliced, 'span', split_axis=0, concat_axis=0, tiled=True)]
    reshape x7 -> x2, local copies, waits for them, and re-layouts: 28.6 us -> 0.94 us  [the longest x1 0.69 us: fused(): qkv_weight.reshape(kept, -1)]
    all_to_all x2 -> x0, waiting for transfers between devices: 18.9 us -> none  [prefix(): lax.all_to_all(earlier, 'span', split_axis=0, concat_axis=0, tiled=True)]
    unnamed x15 -> x10, local copies, waits for them, and re-layouts: 15.9 us -> 0.94 us
    dot_general x5 -> x0, matrix products: 14 us -> none  [the longest x1 4.7 us: project(): projected = jnp.dot(normed, w_qkv, preferred_element_type=jnp.float32)]
  transfers between devices with their start and end apart: 5 -> 0, of which waited for: 5 -> 0; matrix products, arithmetic and copies ran while one was open for 1% -> 0% of each run, Pallas kernels for 0% -> 0%
where the time goes in v1:
time: 135 us
  Pallas kernels  122 us (90%)
  other arithmetic  10.7 us (8%)
  local copies, waits for them, and re-layouts  1.91 us (1%)
    pallas_call x1, Pallas kernels, fused(): pl.pallas_call(layers_kernel, out_shape=jax.ShapeDtypeStruct((2, padded,...  122 us
    unnamed x2, other arithmetic  9.83 us

profile of v1, /device:TPU:5, one launch (start us, length us, event | category | flops | bytes accessed | tf_op | source)
XLA Modules:
  0.0 134.9 jit_solution(527334575999430615)
XLA Ops:
  0.0 8.9 %reduce = bf16[235200]{0:T(1024)(128)(2,1)S(1)} reduce(bf16[1,235200]{1,0:T(2,128)(2,1)} %param.9, bf16[]{:T(256)} %constant.6), dimensions={0}, to_apply=%param.9.reduce_sub_computation | reduce | bytes 940802 | tf_op args[3]
  8.9 0.0 copy-start.4
  8.9 0.7 reshape.10.qkv_ref
  9.6 0.3 copy-done.4
  9.9 0.0 copy-start
  9.9 1.0 reduce.1
  10.8 0.0 copy-start.1
  10.8 0.0 copy-start.2
  10.8 0.2 reshape.11.out_w_ref
  11.1 0.0 copy-start.3
  11.1 0.0 copy-done
  11.1 0.4 copy-done.1
  11.5 0.0 copy-done.2
  11.5 0.2 copy-done.3
  11.8 122.3 %shard_map.64 = bf16[2,144,640]{2,1,0:T(8,128)(2,1)S(1)} custom-call(bf16[136,1120]{1,0:T(8,128)(2,1)S(1)} %copy-done, s32[1,136]{1,0:T(1,128)S(1)} %bitcast.7, f32[1,1120]{1,0:T(1,128)S(1)} %copy-done.1, bf16[70,3360]{1,0:T(8,128)(2,1)S(1)} %reshape.10.qkv_ref, f32[1,1120]{1,0:T(1,128)S(1)} %copy-done.2, bf16[70,1120]{1,0:T(8,128)(2,1)S(1)} %reshape.11.out_w_ref), custom_call_target="tpu_custom_call" | custom-call | tf_op jit(solution)/shard_map/pallas_call | solution.py:480
  134.1 0.8 maximum_bitcast_fusion
  (1 shorter events, 0.0 us)
Async XLA Ops:
  8.9 1.0 copy-start.4
  9.9 1.2 copy-start
  10.8 0.7 copy-start.1
  10.8 0.7 copy-start.2
  11.1 0.7 copy-start.3

commit v2 on v1

--- a/solution.py
+++ b/solution.py
@@ -140,11 +140,11 @@
     )
 
 
-def spread(size_in, size_out, group_in, kept_in, group_out, kept_out):
-    row = lax.broadcasted_iota(jnp.int32, (size_in, size_out), 0)
+def spread(size_in, size_out, group_in, kept_in, group_out, kept_out, skipped=0):
+    row = lax.broadcasted_iota(jnp.int32, (size_in, size_out), 0) + (group_in - skipped)
     col = lax.broadcasted_iota(jnp.int32, (size_in, size_out), 1)
     row_in, col_in = row % group_in, col % group_out
-    row_feature = row // group_in * kept_in + row_in
+    row_feature = (row // group_in - 1) * kept_in + row_in
     col_feature = col // group_out * kept_out + col_in
     same = (row_feature == col_feature) & (row_in < kept_in) & (col_in < kept_out)
     return jnp.where(same, 1.0, 0.0).astype(jnp.bfloat16)
@@ -152,9 +152,9 @@
 
 def layers_kernel(
     x_ref, frame_ref, norm_ref, qkv_ref, head_ref, out_w_ref, y_ref,
-    held, packed, stream, normed, queries, keys, values, mixed, attended, fresh,
+    held_a, held_b, held_out, packed, packed_out, got, got_out, stream, normed, projected, queries, keys, values, mixed, attended, fresh,
     state, sent_state, got_state, sent_sum, got_sum,
-    frames, masks, norm_scale, head_scale, to_shards, from_heads,
+    frames, masks, norm_scale, head_scale, to_blocks, from_heads, to_heads,
     gather_send, gather_recv, pair_send, pair_recv, state_send, state_recv,
     sum_send, sum_recv, y_send, y_recv, local_sem,
 ):
@@ -169,7 +169,8 @@
     x_near = span + 2 - 4 * x_at
     chips = got_state.shape[0]
     z_count = chips // 2
-    shards, shard_rows = held.shape[0], held.shape[1]
+    block_rows = held_a.shape[1]
+    cut_at, window = held_a.shape[2], to_heads.shape[1]
     rows = x_ref.shape[0]
     padded = stream.shape[1] // 2
     half_width = x_ref.shape[1] // 2
@@ -198,83 +199,109 @@
     )
 
     packed[...] = jnp.zeros_like(packed)
+    packed_out[...] = jnp.zeros_like(packed_out)
     for part in range(2):
         for third in range(3):
-            for head in range(heads):
-                at = third * width + part * half_width + head * HEAD
-                to = (third * heads + head) * LANES
-                packed[part, 0:kept, to : to + HEAD] = qkv_ref[:, at : at + HEAD]
-        to = 3 * heads * LANES
-        packed[part, 0:kept, to : to + half_width] = out_w_ref[
+            at = third * width + part * half_width
+            to = third * half_width
+            packed[part, 0:kept, to : to + half_width] = qkv_ref[:, at : at + half_width]
+        packed_out[part, 0:kept, 0:half_width] = out_w_ref[
             :, part * half_width : (part + 1) * half_width
         ]
 
     pl.semaphore_wait(barrier, chips + 1)
 
-    own = pltpu.make_async_copy(packed.at[core], held.at[span], local_sem)
-    own.start()
-    give = remote(packed.at[1 - core], held.at[span], pair_send.at[0], gather_recv.at[span], pair, section)
+    give = remote(packed.at[1 - core], got, pair_send.at[0], pair_recv.at[0], pair, section)
     give.start()
+    give_out = remote(packed_out.at[1 - core], got_out, pair_send.at[5], pair_recv.at[5], pair, section)
+    give_out.start()
     give_frames = remote(frames.at[core], frames.at[core], pair_send.at[1], pair_recv.at[1], pair, section)
     give_frames.start()
-    own.wait()
-
-    def forward(lane, shard, target):
+
+    here = pl.ds(chip, 1)
+    pieces = (held_a, held_b, held_out)
+    for piece_ref in pieces:
+        piece_ref[here, 2 * kept : block_rows, :] = jnp.zeros(
+            (1, block_rows - 2 * kept, piece_ref.shape[2]), bf16
+        )
+    give.wait_recv()
+    for which in range(2):
+
+        @pl.when(core == which)
+        def _():
+            a, b = slice(which * kept, (which + 1) * kept), slice((1 - which) * kept, (2 - which) * kept)
+            held_a[here, a, :] = packed[which, 0:kept, 0:cut_at][None]
+            held_a[here, b, :] = got[0:kept, 0:cut_at][None]
+            held_b[here, a, :] = packed[which, 0:kept, cut_at:][None]
+            held_b[here, b, :] = got[0:kept, cut_at:][None]
+
+    def forward(piece, lane, block, target):
         return remote(
-            held.at[shard], held.at[shard], gather_send.at[lane, shard], gather_recv.at[shard],
+            pieces[piece].at[block], pieces[piece].at[block],
+            gather_send.at[piece * 3 + lane, block], gather_recv.at[piece, block],
             target, section,
         )
 
-    def arrival(shard):
-        return remote(
-            held.at[shard], held.at[shard], gather_send.at[0, shard], gather_recv.at[shard],
-            pair, section,
-        )
-
-    def pass_on(step, from_core, first):
+    def pass_on(piece, step):
         if step == 0:
-            shard = z_at * 4 + x_at * 2 + from_core
-            if not first:
-                arrival(shard).wait_recv()
 
             @pl.when(z_at < z_count - 1)
             def _():
-                forward(0, shard, span + 4).start()
+                forward(piece, 0, chip, span + 4).start()
 
             @pl.when(z_at > 0)
             def _():
-                forward(1, shard, span - 4).start()
-
-            forward(2, shard, x_near).start()
+                forward(piece, 1, chip, span - 4).start()
+
+            forward(piece, 2, chip, x_near).start()
         else:
-            below = (z_at - step) * 4 + x_at * 2 + from_core
-            above = (z_at + step) * 4 + x_at * 2 + from_core
+            below = (z_at - step) * 2 + x_at
+            above = (z_at + step) * 2 + x_at
 
             @pl.when(z_at >= step)
             def _():
-                arrival(below).wait_recv()
+                forward(piece, 2, below, x_near).wait_recv()
 
                 @pl.when(z_at < z_count - 1)
                 def _():
-                    forward(0, below, span + 4).start()
-
-                forward(2, below, x_near).start()
+                    forward(piece, 0, below, span + 4).start()
+
+                forward(piece, 2, below, x_near).start()
 
             @pl.when(z_at + step < z_count)
             def _():
-                arrival(above).wait_recv()
+                forward(piece, 2, above, x_near).wait_recv()
 
                 @pl.when(z_at > 0)
                 def _():
-                    forward(1, above, span - 4).start()
-
-                forward(2, above, x_near).start()
-
-    pass_on(0, core, True)
-    pass_on(0, 1 - core, False)
-
-    to_shards[...] = spread(half_lanes, half_lanes, half_lanes, half_width, shard_rows, kept)
-    from_heads[...] = spread(half_lanes, half_lanes, LANES, HEAD, shard_rows, kept)
+                    forward(piece, 1, above, span - 4).start()
+
+                forward(piece, 2, above, x_near).start()
+
+    def last_arrivals(piece):
+        for z_from in range(z_count):
+            forward(piece, 2, z_from * 2 + (1 - x_at), x_near).wait_recv()
+
+    pass_on(0, 0)
+    pass_on(1, 0)
+
+    give_out.wait_recv()
+    for which in range(2):
+
+        @pl.when(core == which)
+        def _():
+            a, b = slice(which * kept, (which + 1) * kept), slice((1 - which) * kept, (2 - which) * kept)
+            held_out[here, a, :] = packed_out[which, 0:kept, :][None]
+            held_out[here, b, :] = got_out[0:kept, :][None]
+
+    block_lanes = normed.shape[2]
+    to_blocks[...] = spread(half_lanes, block_lanes, half_lanes, half_width, block_rows, 2 * kept)
+    from_heads[...] = spread(heads * LANES, block_lanes, LANES, HEAD, block_rows, 2 * kept)
+    window_at = [third * half_width // LANES * LANES for third in range(3)]
+    for third in range(3):
+        to_heads[third] = spread(
+            window, heads * LANES, window, half_width, LANES, HEAD, third * half_width - window_at[third]
+        )
     norm_scale[...] = jnp.zeros_like(norm_scale)
     for part in range(2):
         norm_scale[part : part + 1, 0:half_width] = norm_ref[
@@ -310,15 +337,16 @@
         share.wait()
 
     for step in range(1, z_count):
-        pass_on(step, core, False)
-        pass_on(step, 1 - core, False)
-
-    for z_from in range(z_count):
-        for from_core in range(2):
-            arrival(z_from * 4 + (1 - x_at) * 2 + from_core).wait_recv()
+        pass_on(0, step)
+        pass_on(1, step)
+    pass_on(2, 0)
+    last_arrivals(0)
+    last_arrivals(1)
 
     @pl.when(section == 1)
     def _():
+        for step in range(1, z_count):
+            pass_on(2, step)
         arrive = remote(
             stream.at[core], stream.at[core], y_send, y_recv, span, 1 - section
         )
@@ -334,15 +362,32 @@
     inverse = lax.rsqrt(square / width + EPS)
     for part in range(2):
         scaled = (wide[part] * inverse * norm_scale[part : part + 1, :]).astype(bf16)
-        normed[:, part * half_lanes : (part + 1) * half_lanes] = jnp.dot(
-            scaled, to_shards[...], preferred_element_type=f32
+        normed[part] = jnp.dot(scaled, to_blocks[...], preferred_element_type=f32).astype(bf16)
+    lanes = heads * LANES
+    half_chips = chips // 2
+
+    def weight_of(ref, part):
+        block = ref[part * half_chips : (part + 1) * half_chips]
+        return block.reshape(half_chips * block_rows, ref.shape[2])
+
+    for index, ref in enumerate((held_a, held_b)):
+        projected[:, index * cut_at : (index + 1) * cut_at] = (
+            jnp.dot(normed[0], weight_of(ref, 0), preferred_element_type=f32)
+            + jnp.dot(normed[1], weight_of(ref, 1), preferred_element_type=f32)
         ).astype(bf16)
-    lanes = heads * LANES
-    depth = shards * shard_rows
     for third, into in ((1, keys), (2, values), (0, queries)):
-        weight = held[:, :, third * lanes : (third + 1) * lanes].reshape(depth, lanes)
-        result = jnp.dot(normed[...], weight, preferred_element_type=f32)
+        result = jnp.dot(
+            projected[:, window_at[third] : window_at[third] + window], to_heads[third],
+            preferred_element_type=f32,
+        )
         into[...] = (result if third == 2 else jnp.maximum(result, 0.0)).astype(bf16)
+
+    def pass_out(step):
+        @pl.when(section == 0)
+        def _():
+            pass_on(2, step)
+
+    pass_out(1)
 
     contract_rows = (((0,), (0,)), ((), ()))
     for which in range(2):
@@ -386,6 +431,7 @@
             mixed[at, cols] = jnp.dot(scores, values[at, cols], preferred_element_type=f32)
 
     local_part(0)
+    pass_out(2)
     for step in range(1, chips):
         landed(got_state, state_send, state_recv, step).wait_recv()
     running = jnp.zeros((piece, LANES), f32)
@@ -396,6 +442,7 @@
         exchange(sent_sum, got_sum, sum_send, sum_recv, step).start()
     got_sum[pl.ds(chip, 1)] = sent_sum[pl.ds(chip, 1)]
     local_part(1)
+    pass_out(3)
     for step in range(1, chips):
         landed(got_sum, sum_send, sum_recv, step).wait_recv()
 
@@ -420,13 +467,10 @@
     swap.start()
     swap.wait()
 
-    half_depth = depth // 2
+    last_arrivals(2)
     total = stream[pl.ds(core, 1)].astype(f32)[0]
     for part in range(2):
-        weight = held[
-            part * (shards // 2) : (part + 1) * (shards // 2), :, 3 * lanes : 3 * lanes + half_lanes
-        ].reshape(half_depth, half_lanes)
-        total = total + jnp.dot(attended[part], weight, preferred_element_type=f32)
+        total = total + jnp.dot(attended[part], weight_of(held_out, part), preferred_element_type=f32)
     mixed_out = total.astype(bf16)
     keys[...] = mixed_out
 
@@ -449,18 +493,19 @@
     for step in range(1, chips):
         exchange(sent_state, got_state, state_send, state_recv, step).wait_send()
         exchange(sent_sum, got_sum, sum_send, sum_recv, step).wait_send()
-    for z_from in range(z_count):
-        for from_core in range(2):
-            shard = z_from * 4 + x_at * 2 + from_core
-            forward(2, shard, x_near).wait_send()
+    give_out.wait_send()
+    for piece in range(3):
+        for z_from in range(z_count):
+            block = z_from * 2 + x_at
+            forward(piece, 2, block, x_near).wait_send()
 
             @pl.when((z_from <= z_at) & (z_at < z_count - 1))
             def _():
-                forward(0, shard, span + 4).wait_send()
+                forward(piece, 0, block, span + 4).wait_send()
 
             @pl.when((z_from >= z_at) & (z_at > 0))
             def _():
-                forward(1, shard, span - 4).wait_send()
+                forward(piece, 1, block, span - 4).wait_send()
 
 
 def fused(clip_tokens, frame_ids, norm_gain, qkv_weight, head_gain, out_weight):
@@ -474,6 +519,10 @@
     half_lanes = whole_tiles(half_width, LANES)
     lanes = heads * LANES
     chips = shards // 2
+    block_rows = whole_tiles(2 * kept, 16)
+    block_lanes = chips // 2 * block_rows
+    cut_at = whole_tiles(3 * half_width, 2 * LANES) // 2
+    window = half_lanes + LANES
     bf16, f32 = jnp.bfloat16, jnp.float32
     dma = pltpu.SemaphoreType.DMA
     vmem = pl.BlockSpec(memory_space=pltpu.VMEM)
@@ -483,15 +532,21 @@
         in_specs=[vmem] * 6,
         out_specs=vmem,
         scratch_shapes=[
-            pltpu.VMEM((shards, shard_rows, 3 * lanes + half_lanes), bf16),
-            pltpu.VMEM((2, shard_rows, 3 * lanes + half_lanes), bf16),
+            pltpu.VMEM((chips, block_rows, cut_at), bf16),
+            pltpu.VMEM((chips, block_rows, cut_at), bf16),
+            pltpu.VMEM((chips, block_rows, half_lanes), bf16),
+            pltpu.VMEM((2, shard_rows, 2 * cut_at), bf16),
+            pltpu.VMEM((2, shard_rows, half_lanes), bf16),
+            pltpu.VMEM((shard_rows, 2 * cut_at), bf16),
+            pltpu.VMEM((shard_rows, half_lanes), bf16),
             pltpu.VMEM((2, 2 * padded, half_lanes), bf16),
-            pltpu.VMEM((2 * padded, shards * shard_rows), bf16),
+            pltpu.VMEM((2, 2 * padded, block_lanes), bf16),
+            pltpu.VMEM((2 * padded, 2 * cut_at), bf16),
             pltpu.VMEM((2 * padded, lanes), bf16),
             pltpu.VMEM((2 * padded, lanes), bf16),
             pltpu.VMEM((2 * padded, lanes), bf16),
             pltpu.VMEM((2 * padded, lanes), f32),
-            pltpu.VMEM((2, 2 * padded, half_lanes), bf16),
+            pltpu.VMEM((2, 2 * padded, block_lanes), bf16),
             pltpu.VMEM((2, padded, half_lanes), bf16),
             pltpu.VMEM((2, lanes, LANES), f32),
             pltpu.VMEM((chips, lanes // chips, LANES), bf16),
@@ -502,12 +557,13 @@
             pltpu.VMEM((2, padded, padded), f32),
             pltpu.VMEM((8, half_lanes), f32),
             pltpu.VMEM((whole_tiles(2 * heads, 8), LANES), f32),
-            pltpu.VMEM((half_lanes, half_lanes), bf16),
-            pltpu.VMEM((lanes, half_lanes), bf16),
-            dma((3, shards)),
-            dma((shards,)),
-            dma((5,)),
-            dma((5,)),
+            pltpu.VMEM((half_lanes, block_lanes), bf16),
+            pltpu.VMEM((lanes, block_lanes), bf16),
+            pltpu.VMEM((3, window, lanes), bf16),
+            dma((9, chips)),
+            dma((3, chips)),
+            dma((6,)),
+            dma((6,)),
             dma((chips,)),
             dma((chips,)),
             dma((chips,)),

time: 135 us -> 121 us (0.90)
  Pallas kernels: 122 us -> 108 us
    pallas_call x1, Pallas kernels: 122 us -> 108 us  [fused(): pl.pallas_call(layers_kernel, out_shape=jax.ShapeDtypeStruct((2, padded,...]
where the time goes in v2:
time: 121 us
  Pallas kernels  108 us (89%)
  other arithmetic  10.7 us (9%)
  local copies, waits for them, and re-layouts  1.91 us (2%)
    pallas_call x1, Pallas kernels, fused(): pl.pallas_call(layers_kernel, out_shape=jax.ShapeDtypeStruct((2, padded,...  108 us
    unnamed x2, other arithmetic  9.83 us

profile of v2, /device:TPU:5, one launch (start us, length us, event | category | flops | bytes accessed | tf_op | source)
XLA Modules:
  0.0 121.1 jit_solution(13260913354333017043)
XLA Ops:
  0.0 8.9 %reduce = bf16[235200]{0:T(1024)(128)(2,1)S(1)} reduce(bf16[1,235200]{1,0:T(2,128)(2,1)} %param.9, bf16[]{:T(256)} %constant.6), dimensions={0}, to_apply=%param.9.reduce_sub_computation | reduce | bytes 940802 | tf_op args[3]
  8.9 0.0 copy-start.4
  8.9 0.7 reshape.10.qkv_ref
  9.6 0.3 copy-done.4
  9.9 0.0 copy-start
  9.9 1.0 reduce.1
  10.8 0.0 copy-start.1
  10.8 0.0 copy-start.2
  10.8 0.2 reshape.11.out_w_ref
  11.1 0.0 copy-start.3
  11.1 0.0 copy-done
  11.1 0.4 copy-done.1
  11.5 0.0 copy-done.2
  11.5 0.2 copy-done.3
  11.8 108.5 %shard_map.64 = bf16[2,144,640]{2,1,0:T(8,128)(2,1)S(1)} custom-call(bf16[136,1120]{1,0:T(8,128)(2,1)S(1)} %copy-done, s32[1,136]{1,0:T(1,128)S(1)} %bitcast.7, f32[1,1120]{1,0:T(1,128)S(1)} %copy-done.1, bf16[70,3360]{1,0:T(8,128)(2,1)S(1)} %reshape.10.qkv_ref, f32[1,1120]{1,0:T(1,128)S(1)} %copy-done.2, bf16[70,1120]{1,0:T(8,128)(2,1)S(1)} %reshape.11.out_w_ref), custom_call_target="tpu_custom_call" | custom-call | tf_op jit(solution)/shard_map/pallas_call | solution.py:529
  120.3 0.8 maximum_bitcast_fusion
  (1 shorter events, 0.0 us)
Async XLA Ops:
  8.9 1.0 copy-start.4
  9.9 1.2 %copy-start = (bf16[136,1120]{1,0:T(8,128)(2,1)S(1)}, bf16[136,1120]{1,0:T(8,128)(2,1)}, u32[]{:S(2)}) copy-start(bf16[136,1120]{1,0:T(8,128)(2,1)} %x_ref.1) | copy-start | bytes 913924
  10.8 0.7 copy-start.1
  10.8 0.7 copy-start.2
  11.1 0.7 copy-start.3

commit v3 on v2

--- a/solution.py
+++ b/solution.py
@@ -152,10 +152,10 @@
 
 def layers_kernel(
     x_ref, frame_ref, norm_ref, qkv_ref, head_ref, out_w_ref, y_ref,
-    held_a, held_b, held_out, packed, packed_out, got, got_out, stream, normed, projected, queries, keys, values, mixed, attended, fresh,
+    held_a, held_b, held_out, relay, packed, packed_out, got, got_out, stream, normed, projected, queries, keys, values, mixed, attended, fresh,
     state, sent_state, got_state, sent_sum, got_sum,
     frames, masks, norm_scale, head_scale, to_blocks, from_heads, to_heads,
-    gather_send, gather_recv, pair_send, pair_recv, state_send, state_recv,
+    gather_send, gather_recv, hop_send, hop_recv, pair_send, pair_recv, state_send, state_recv,
     sum_send, sum_recv, y_send, y_recv, local_sem,
 ):
     f32, bf16 = jnp.float32, jnp.bfloat16
@@ -219,8 +219,8 @@
     give_frames.start()
 
     here = pl.ds(chip, 1)
-    pieces = (held_a, held_b, held_out)
-    for piece_ref in pieces:
+    pieces = (held_a, held_b, held_out, relay)
+    for piece_ref in pieces[:3]:
         piece_ref[here, 2 * kept : block_rows, :] = jnp.zeros(
             (1, block_rows - 2 * kept, piece_ref.shape[2]), bf16
         )
@@ -282,8 +282,49 @@
         for z_from in range(z_count):
             forward(piece, 2, z_from * 2 + (1 - x_at), x_near).wait_recv()
 
-    pass_on(0, 0)
-    pass_on(1, 0)
+    def hop(source, target, block):
+        return remote(
+            source.at[block], target.at[block], hop_send.at[block], hop_recv.at[block],
+            span, 1 - section,
+        )
+
+    def hop_back(step):
+        if step > 0:
+
+            @pl.when(z_at >= step)
+            def _():
+                hop(relay, held_b, (z_at - step) * 2 + x_at).start()
+
+            @pl.when(z_at + step < z_count)
+            def _():
+                hop(relay, held_b, (z_at + step) * 2 + x_at).start()
+
+        near = 1 - x_at
+
+        @pl.when(z_at >= step)
+        def _():
+            block = (z_at - step) * 2 + near
+            forward(3, 2, block, x_near).wait_recv()
+            hop(relay, held_b, block).start()
+
+        if step > 0:
+
+            @pl.when(z_at + step < z_count)
+            def _():
+                block = (z_at + step) * 2 + near
+                forward(3, 2, block, x_near).wait_recv()
+                hop(relay, held_b, block).start()
+
+    @pl.when(section == 0)
+    def _():
+        hop(held_b, relay, chip).start()
+        pass_on(0, 0)
+
+    @pl.when(section == 1)
+    def _():
+        hop(held_b, relay, chip).wait_recv()
+        pass_on(3, 0)
+        pass_on(0, 0)
 
     give_out.wait_recv()
     for which in range(2):
@@ -336,12 +377,28 @@
         put.wait()
         share.wait()
 
-    for step in range(1, z_count):
-        pass_on(0, step)
-        pass_on(1, step)
-    pass_on(2, 0)
-    last_arrivals(0)
-    last_arrivals(1)
+    @pl.when(section == 0)
+    def _():
+        for step in range(1, z_count):
+            pass_on(0, step)
+        pass_on(2, 0)
+        last_arrivals(0)
+        for step in range(1, chips):
+            hop(relay, held_b, (chip + step) % chips).wait_recv()
+
+    @pl.when(section == 1)
+    def _():
+        for step in range(1, z_count):
+            pass_on(3, step)
+            hop_back(step - 1)
+        pass_on(1, 0)
+        hop_back(z_count - 1)
+        for step in range(1, z_count):
+            pass_on(0, step)
+            pass_on(1, step)
+        pass_on(2, 0)
+        last_arrivals(0)
+        last_arrivals(1)
 
     @pl.when(section == 1)
     def _():
@@ -370,8 +427,8 @@
         block = ref[part * half_chips : (part + 1) * half_chips]
         return block.reshape(half_chips * block_rows, ref.shape[2])
 
-    for index, ref in enumerate((held_a, held_b)):
-        projected[:, index * cut_at : (index + 1) * cut_at] = (
+    for ref, lo, hi in ((held_a, 0, cut_at), (held_b, cut_at, projected.shape[1])):
+        projected[:, lo:hi] = (
             jnp.dot(normed[0], weight_of(ref, 0), preferred_element_type=f32)
             + jnp.dot(normed[1], weight_of(ref, 1), preferred_element_type=f32)
         ).astype(bf16)
@@ -494,7 +551,7 @@
         exchange(sent_state, got_state, state_send, state_recv, step).wait_send()
         exchange(sent_sum, got_sum, sum_send, sum_recv, step).wait_send()
     give_out.wait_send()
-    for piece in range(3):
+    def sends_end(piece):
         for z_from in range(z_count):
             block = z_from * 2 + x_at
             forward(piece, 2, block, x_near).wait_send()
@@ -506,6 +563,20 @@
             @pl.when((z_from >= z_at) & (z_at > 0))
             def _():
                 forward(piece, 1, block, span - 4).wait_send()
+
+    sends_end(0)
+    sends_end(2)
+
+    @pl.when(section == 0)
+    def _():
+        hop(held_b, relay, chip).wait_send()
+
+    @pl.when(section == 1)
+    def _():
+        sends_end(1)
+        sends_end(3)
+        for step in range(1, chips):
+            hop(relay, held_b, (chip + step) % chips).wait_send()
 
 
 def fused(clip_tokens, frame_ids, norm_gain, qkv_weight, head_gain, out_weight):
@@ -521,7 +592,8 @@
     chips = shards // 2
     block_rows = whole_tiles(2 * kept, 16)
     block_lanes = chips // 2 * block_rows
-    cut_at = whole_tiles(3 * half_width, 2 * LANES) // 2
+    qkv_lanes = whole_tiles(3 * half_width, LANES)
+    cut_at = qkv_lanes // LANES * 9 // 14 * LANES
     window = half_lanes + LANES
     bf16, f32 = jnp.bfloat16, jnp.float32
     dma = pltpu.SemaphoreType.DMA
@@ -533,15 +605,16 @@
         out_specs=vmem,
         scratch_shapes=[
             pltpu.VMEM((chips, block_rows, cut_at), bf16),
-            pltpu.VMEM((chips, block_rows, cut_at), bf16),
+            pltpu.VMEM((chips, block_rows, qkv_lanes - cut_at), bf16),
             pltpu.VMEM((chips, block_rows, half_lanes), bf16),
-            pltpu.VMEM((2, shard_rows, 2 * cut_at), bf16),
+            pltpu.VMEM((chips, block_rows, qkv_lanes - cut_at), bf16),
+            pltpu.VMEM((2, shard_rows, qkv_lanes), bf16),
             pltpu.VMEM((2, shard_rows, half_lanes), bf16),
-            pltpu.VMEM((shard_rows, 2 * cut_at), bf16),
+            pltpu.VMEM((shard_rows, qkv_lanes), bf16),
             pltpu.VMEM((shard_rows, half_lanes), bf16),
             pltpu.VMEM((2, 2 * padded, half_lanes), bf16),
             pltpu.VMEM((2, 2 * padded, block_lanes), bf16),
-            pltpu.VMEM((2 * padded, 2 * cut_at), bf16),
+            pltpu.VMEM((2 * padded, qkv_lanes), bf16),
             pltpu.VMEM((2 * padded, lanes), bf16),
             pltpu.VMEM((2 * padded, lanes), bf16),
             pltpu.VMEM((2 * padded, lanes), bf16),
@@ -560,8 +633,10 @@
             pltpu.VMEM((half_lanes, block_lanes), bf16),
             pltpu.VMEM((lanes, block_lanes), bf16),
             pltpu.VMEM((3, window, lanes), bf16),
-            dma((9, chips)),
-            dma((3, chips)),
+            dma((12, chips)),
+            dma((4, chips)),
+            dma((chips,)),
+            dma((chips,)),
             dma((6,)),
             dma((6,)),
             dma((chips,)),

time: 121 us -> 123 us (1.017)
  Pallas kernels: 108 us -> 110 us
    pallas_call x1, Pallas kernels: 108 us -> 110 us  [fused(): pl.pallas_call(layers_kernel, out_shape=jax.ShapeDtypeStruct((2, padded,...]
where the time goes in v3:
time: 123 us
  Pallas kernels  110 us (89%)
  other arithmetic  10.7 us (9%)
  local copies, waits for them, and re-layouts  1.91 us (2%)
    pallas_call x1, Pallas kernels, fused(): pl.pallas_call(layers_kernel, out_shape=jax.ShapeDtypeStruct((2, padded,...  110 us
    unnamed x2, other arithmetic  9.83 us

profile of v3, /device:TPU:5, one launch (start us, length us, event | category | flops | bytes accessed | tf_op | source)
XLA Modules:
  0.0 122.7 jit_solution(3800341701176685268)
XLA Ops:
  0.0 8.9 %reduce = bf16[235200]{0:T(1024)(128)(2,1)S(1)} reduce(bf16[1,235200]{1,0:T(2,128)(2,1)} %param.9, bf16[]{:T(256)} %constant.6), dimensions={0}, to_apply=%param.9.reduce_sub_computation | reduce | bytes 940802 | tf_op args[3]
  8.9 0.0 copy-start.4
  8.9 0.7 reshape.10.qkv_ref
  9.6 0.3 copy-done.4
  9.9 0.0 copy-start
  9.9 1.0 reduce.1
  10.8 0.0 copy-start.1
  10.8 0.0 copy-start.2
  10.8 0.2 reshape.11.out_w_ref
  11.1 0.0 copy-start.3
  11.1 0.0 copy-done
  11.1 0.4 copy-done.1
  11.5 0.0 copy-done.2
  11.5 0.2 copy-done.3
  11.8 110.0 %shard_map.64 = bf16[2,144,640]{2,1,0:T(8,128)(2,1)S(1)} custom-call(bf16[136,1120]{1,0:T(8,128)(2,1)S(1)} %copy-done, s32[1,136]{1,0:T(1,128)S(1)} %bitcast.7, f32[1,1120]{1,0:T(1,128)S(1)} %copy-done.1, bf16[70,3360]{1,0:T(8,128)(2,1)S(1)} %reshape.10.qkv_ref, f32[1,1120]{1,0:T(1,128)S(1)} %copy-done.2, bf16[70,1120]{1,0:T(8,128)(2,1)S(1)} %reshape.11.out_w_ref), custom_call_target="tpu_custom_call" | custom-call | tf_op jit(solution)/shard_map/pallas_call | solution.py:601
  121.8 0.8 maximum_bitcast_fusion
  (1 shorter events, 0.0 us)
Async XLA Ops:
  8.9 1.0 copy-start.4
  9.9 1.2 %copy-start = (bf16[136,1120]{1,0:T(8,128)(2,1)S(1)}, bf16[136,1120]{1,0:T(8,128)(2,1)}, u32[]{:S(2)}) copy-start(bf16[136,1120]{1,0:T(8,128)(2,1)} %x_ref.1) | copy-start | bytes 913924
  10.8 0.7 copy-start.1
  10.8 0.7 copy-start.2
  11.1 0.7 copy-start.3

commit v4 on v2

--- a/solution.py
+++ b/solution.py
@@ -141,12 +141,12 @@
 
 
 def spread(size_in, size_out, group_in, kept_in, group_out, kept_out, skipped=0):
-    row = lax.broadcasted_iota(jnp.int32, (size_in, size_out), 0) + (group_in - skipped)
-    col = lax.broadcasted_iota(jnp.int32, (size_in, size_out), 1)
+    row = lax.broadcasted_iota(jnp.int32, (size_in, 1), 0) + (group_in - skipped)
+    col = lax.broadcasted_iota(jnp.int32, (1, size_out), 1)
     row_in, col_in = row % group_in, col % group_out
-    row_feature = (row // group_in - 1) * kept_in + row_in
-    col_feature = col // group_out * kept_out + col_in
-    same = (row_feature == col_feature) & (row_in < kept_in) & (col_in < kept_out)
+    row_feature = jnp.where(row_in < kept_in, (row // group_in - 1) * kept_in + row_in, -1)
+    col_feature = jnp.where(col_in < kept_out, col // group_out * kept_out + col_in, -2)
+    same = jnp.broadcast_to(row_feature, (size_in, size_out)) == col_feature
     return jnp.where(same, 1.0, 0.0).astype(jnp.bfloat16)
 
 

time: 121 us -> 121 us (level)
  no operation moved by 1% of the time
where the time goes in v4:
time: 121 us
  Pallas kernels  108 us (89%)
  other arithmetic  10.7 us (9%)
  local copies, waits for them, and re-layouts  1.91 us (2%)
    pallas_call x1, Pallas kernels, fused(): pl.pallas_call(layers_kernel, out_shape=jax.ShapeDtypeStruct((2, padded,...  108 us
    unnamed x2, other arithmetic  9.83 us

profile of v4, /device:TPU:5, one launch (start us, length us, event | category | flops | bytes accessed | tf_op | source)
XLA Modules:
  0.0 121.1 jit_solution(18143543314166976347)
XLA Ops:
  0.0 8.9 %reduce = bf16[235200]{0:T(1024)(128)(2,1)S(1)} reduce(bf16[1,235200]{1,0:T(2,128)(2,1)} %param.9, bf16[]{:T(256)} %constant.6), dimensions={0}, to_apply=%param.9.reduce_sub_computation | reduce | bytes 940802 | tf_op args[3]
  8.9 0.0 copy-start.4
  8.9 0.7 reshape.10.qkv_ref
  9.6 0.3 copy-done.4
  9.9 0.0 copy-start
  9.9 1.0 reduce.1
  10.8 0.0 copy-start.1
  10.8 0.0 copy-start.2
  10.8 0.2 reshape.11.out_w_ref
  11.1 0.0 copy-start.3
  11.1 0.0 copy-done
  11.1 0.4 copy-done.1
  11.5 0.0 copy-done.2
  11.5 0.2 copy-done.3
  11.8 108.5 %shard_map.64 = bf16[2,144,640]{2,1,0:T(8,128)(2,1)S(1)} custom-call(bf16[136,1120]{1,0:T(8,128)(2,1)S(1)} %copy-done, s32[1,136]{1,0:T(1,128)S(1)} %bitcast.7, f32[1,1120]{1,0:T(1,128)S(1)} %copy-done.1, bf16[70,3360]{1,0:T(8,128)(2,1)S(1)} %reshape.10.qkv_ref, f32[1,1120]{1,0:T(1,128)S(1)} %copy-done.2, bf16[70,1120]{1,0:T(8,128)(2,1)S(1)} %reshape.11.out_w_ref), custom_call_target="tpu_custom_call" | custom-call | tf_op jit(solution)/shard_map/pallas_call | solution.py:529
  120.3 0.8 maximum_bitcast_fusion
  (1 shorter events, 0.0 us)
Async XLA Ops:
  8.9 1.0 copy-start.4
  9.9 1.2 %copy-start = (bf16[136,1120]{1,0:T(8,128)(2,1)S(1)}, bf16[136,1120]{1,0:T(8,128)(2,1)}, u32[]{:S(2)}) copy-start(bf16[136,1120]{1,0:T(8,128)(2,1)} %x_ref.1) | copy-start | bytes 913924
  10.8 0.7 copy-start.1
  10.8 0.7 copy-start.2
  11.1 0.7 copy-start.3

commit v5 on v4

--- a/solution.py
+++ b/solution.py
@@ -205,14 +205,15 @@
             at = third * width + part * half_width
             to = third * half_width
             packed[part, 0:kept, to : to + half_width] = qkv_ref[:, at : at + half_width]
+
+    pl.semaphore_wait(barrier, chips + 1)
+
+    give = remote(packed.at[1 - core], got, pair_send.at[0], pair_recv.at[0], pair, section)
+    give.start()
+    for part in range(2):
         packed_out[part, 0:kept, 0:half_width] = out_w_ref[
             :, part * half_width : (part + 1) * half_width
         ]
-
-    pl.semaphore_wait(barrier, chips + 1)
-
-    give = remote(packed.at[1 - core], got, pair_send.at[0], pair_recv.at[0], pair, section)
-    give.start()
     give_out = remote(packed_out.at[1 - core], got_out, pair_send.at[5], pair_recv.at[5], pair, section)
     give_out.start()
     give_frames = remote(frames.at[core], frames.at[core], pair_send.at[1], pair_recv.at[1], pair, section)
@@ -347,15 +348,16 @@
     def _():
         for step in range(1, z_count):
             pass_on(2, step)
-        arrive = remote(
-            stream.at[core], stream.at[core], y_send, y_recv, span, 1 - section
-        )
-        arrive.wait_recv()
-        share = remote(
-            stream.at[core], stream.at[core], pair_send.at[2], pair_recv.at[2], pair, section
-        )
-        share.start()
-        share.wait()
+        shares = []
+        for chunk in range(2):
+            at = stream.at[core, chunk * padded : (chunk + 1) * padded, :]
+            remote(at, at, y_send.at[chunk], y_recv.at[chunk], span, 1 - section).wait_recv()
+            slot = 2 + 4 * chunk
+            share = remote(at, at, pair_send.at[slot], pair_recv.at[slot], pair, section)
+            share.start()
+            shares.append(share)
+        for share in shares:
+            share.wait()
 
     wide = [stream[part].astype(f32) for part in range(2)]
     square = sum(jnp.sum(value * value, axis=1, keepdims=True) for value in wide)
@@ -468,15 +470,26 @@
     swap.wait()
 
     last_arrivals(2)
-    total = stream[pl.ds(core, 1)].astype(f32)[0]
-    for part in range(2):
-        total = total + jnp.dot(attended[part], weight_of(held_out, part), preferred_element_type=f32)
-    mixed_out = total.astype(bf16)
-    keys[...] = mixed_out
-
-    @pl.when(section == 0)
-    def _():
-        remote(keys, stream.at[core], y_send, y_recv, span, 1 - section).start()
+
+    def next_layer(chunk):
+        at = slice(chunk * padded, (chunk + 1) * padded)
+        return remote(
+            keys.at[at, :], stream.at[core, at, :], y_send.at[chunk], y_recv.at[chunk],
+            span, 1 - section,
+        )
+
+    for chunk in range(2):
+        at = slice(chunk * padded, (chunk + 1) * padded)
+        total = stream[pl.ds(core, 1), at, :].astype(f32)[0]
+        for part in range(2):
+            total = total + jnp.dot(
+                attended[part, at, :], weight_of(held_out, part), preferred_element_type=f32
+            )
+        keys[at, :] = total.astype(bf16)
+
+        @pl.when(section == 0)
+        def _():
+            next_layer(chunk).start()
 
     back = remote(keys.at[theirs, :], y_ref.at[core], pair_send.at[4], pair_recv.at[4], pair, section)
     back.start()
@@ -487,7 +500,8 @@
 
     @pl.when(section == 0)
     def _():
-        remote(keys, stream.at[core], y_send, y_recv, span, 1 - section).wait_send()
+        next_layer(0).wait_send()
+        next_layer(1).wait_send()
 
     give.wait_send()
     for step in range(1, chips):
@@ -562,14 +576,14 @@
             pltpu.VMEM((3, window, lanes), bf16),
             dma((9, chips)),
             dma((3, chips)),
-            dma((6,)),
-            dma((6,)),
+            dma((7,)),
+            dma((7,)),
             dma((chips,)),
             dma((chips,)),
             dma((chips,)),
             dma((chips,)),
-            dma,
-            dma,
+            dma((2,)),
+            dma((2,)),
             dma,
         ],
         compiler_params=pltpu.CompilerParams(

time: 121 us -> 121 us (level)
  no operation moved by 1% of the time
where the time goes in v5:
time: 121 us
  Pallas kernels  108 us (89%)
  other arithmetic  10.7 us (9%)
  local copies, waits for them, and re-layouts  1.91 us (2%)
    pallas_call x1, Pallas kernels, fused(): pl.pallas_call(layers_kernel, out_shape=jax.ShapeDtypeStruct((2, padded,...  108 us
    unnamed x2, other arithmetic  9.83 us

profile of v5, /device:TPU:5, one launch (start us, length us, event | category | flops | bytes accessed | tf_op | source)
XLA Modules:
  0.0 120.8 jit_solution(14123375845700780601)
XLA Ops:
  0.0 8.9 %reduce = bf16[235200]{0:T(1024)(128)(2,1)S(1)} reduce(bf16[1,235200]{1,0:T(2,128)(2,1)} %param.9, bf16[]{:T(256)} %constant.6), dimensions={0}, to_apply=%param.9.reduce_sub_computation | reduce | bytes 940802 | tf_op args[3]
  8.9 0.0 copy-start.4
  8.9 0.7 reshape.10.qkv_ref
  9.6 0.3 copy-done.4
  9.9 0.0 copy-start
  9.9 1.0 reduce.1
  10.8 0.0 copy-start.1
  10.8 0.0 copy-start.2
  10.8 0.2 reshape.11.out_w_ref
  11.1 0.0 copy-start.3
  11.1 0.0 copy-done
  11.1 0.4 copy-done.1
  11.5 0.0 copy-done.2
  11.5 0.2 copy-done.3
  11.8 108.1 %shard_map.64 = bf16[2,144,640]{2,1,0:T(8,128)(2,1)S(1)} custom-call(bf16[136,1120]{1,0:T(8,128)(2,1)S(1)} %copy-done, s32[1,136]{1,0:T(1,128)S(1)} %bitcast.7, f32[1,1120]{1,0:T(1,128)S(1)} %copy-done.1, bf16[70,3360]{1,0:T(8,128)(2,1)S(1)} %reshape.10.qkv_ref, f32[1,1120]{1,0:T(1,128)S(1)} %copy-done.2, bf16[70,1120]{1,0:T(8,128)(2,1)S(1)} %reshape.11.out_w_ref), custom_call_target="tpu_custom_call" | custom-call | tf_op jit(solution)/shard_map/pallas_call | solution.py:543
  120.0 0.8 maximum_bitcast_fusion
  (1 shorter events, 0.0 us)
Async XLA Ops:
  8.9 1.0 copy-start.4
  9.9 1.2 %copy-start = (bf16[136,1120]{1,0:T(8,128)(2,1)S(1)}, bf16[136,1120]{1,0:T(8,128)(2,1)}, u32[]{:S(2)}) copy-start(bf16[136,1120]{1,0:T(8,128)(2,1)} %x_ref.1) | copy-start | bytes 913924
  10.8 0.7 copy-start.1
  10.8 0.7 copy-start.2
  11.1 0.7 copy-start.3
